TPU v7x, 32 devices: a whole 2x2x4 slice. The times are simulated.
32 devices in a mesh: freq: 8 (over z, core), tm: 2 (over y), beam: 2 (over x).
Axes of the slice: x: 2, y: 2, z: 4, core: 2. Of those that a mesh axis runs over, the one named last changes fastest.
Arguments:
- raw_samples: bfloat16 [6144, 4096], P(('beam', 'tm'), 'freq'), parts along dimension 0, may hold values from -6 to 6
- filter_taps: bfloat16 [16, 4096], P(None, 'freq'), may hold values from -1.5 to 1.5
- dm_trials: int32 [256], replicated, may hold values from 0 to 1024, as said below
- channel_units: int32 [4096], replicated, may hold values from 0 to 512, as said below
Outputs:
- dm_power: float32 [4, 256, 256], P(('beam', 'tm'), 'freq'), parts along dimension 0
There are 2 independent parts, one for each index of `beam`. A program takes and returns all parts, laid end to end along the dimension named above; an argument that names none is the same for every part. Nothing has to cross between parts.
Inputs may be any that keep to these rules, and one draw needn't show every extreme that they name: Trial d delays a channel of integer delay u by floor(dm_trials[d] * u / 1024) frames. `channel_units`: so that no dispersion delay exceeds 512 frames.
All inputs are finite; a program needn't handle non-finite values.
Results may differ from a plain program's by a relative error of at most 0.0072.
Values may be sent and summed in bfloat16 or wider, within the bound.
A program may use at most 64 MiB of HBM per device.

v0:
```python
import functools
import math

import jax
import jax.numpy as jnp
import numpy as np
from jax import lax
from jax.experimental import pallas as pl
from jax.experimental.pallas import tpu as pltpu
from jax.sharding import PartitionSpec as P

TAPS = 16
DFT_LEN = 2048
BINS = 256
SHARED = 512
DMS = 256
DM_STEPS = 1024
CHANNELS = 4096
RADIX = 8
INNER = CHANNELS // RADIX
CHUNK = 16
LANES = 128


def tables():
    bins = np.arange(BINS)[:, None]
    angle = 2 * np.pi * (bins * np.arange(DFT_LEN)[None, :] % DFT_LEN) / DFT_LEN
    time = np.concatenate([np.cos(angle), -np.sin(angle)], 0) / math.sqrt(DFT_LEN)
    angle = 2 * np.pi * (bins * np.arange(TAPS)[None, :]) / DFT_LEN
    tap = np.concatenate([np.cos(angle), -np.sin(angle)], 0)
    ids = np.arange(INNER)
    angle = 2 * np.pi * (np.arange(RADIX)[:, None] * ids[None, :]) / CHANNELS
    twiddle = np.stack([np.cos(angle), -np.sin(angle)]) / math.sqrt(RADIX)
    spread = ids.reshape(CHANNELS // LANES, LANES // RADIX).T.reshape(-1)
    angle = 2 * np.pi * (ids[:, None] * spread[None, :] % INNER) / INNER
    cosine, sine = np.cos(angle), np.sin(angle)
    channel = np.block([[cosine, -sine], [sine, cosine]]) / math.sqrt(INNER)
    return (
        jnp.asarray(time, jnp.bfloat16),
        jnp.asarray(tap, jnp.float32),
        jnp.asarray(twiddle, jnp.float32),
        jnp.asarray(channel, jnp.bfloat16),
    )


def unit_circle(phase):
    x = phase.astype(jnp.float32) * (2.0 * math.pi / DFT_LEN)
    y = x * x
    sine, cosine = jnp.full_like(y, -1 / 39916800), jnp.full_like(y, 1 / 479001600)
    for value in (1 / 362880, -1 / 5040, 1 / 120, -1 / 6, 1.0):
        sine = sine * y + value
    for value in (-1 / 3628800, 1 / 40320, -1 / 720, 1 / 24, -0.5, 1.0):
        cosine = cosine * y + value
    return cosine, sine * x


def fill_ramps(ramps, dms, first_bin, start, stop):
    bins = ramps.shape[0]

    @pl.loop(start, stop)
    def _(step):
        row = pl.multiple_of(step * CHUNK, CHUNK)
        units = lax.broadcasted_iota(jnp.int32, (CHUNK, DMS), 0) + (row + 1)
        delays = (units * dms[...]) >> 10
        turn_cos, turn_sin = unit_circle(delays)
        phase = (delays * first_bin) & (DFT_LEN - 1)
        quarter = phase >> 9
        cosine, sine = unit_circle(phase & 511)
        odd = (quarter & 1) == 1
        swapped_cos = jnp.where(odd, -sine, cosine)
        swapped_sin = jnp.where(odd, cosine, sine)
        far = quarter >= 2
        cosine = jnp.where(far, -swapped_cos, swapped_cos)
        sine = jnp.where(far, -swapped_sin, swapped_sin)
        for at in range(bins):
            ramps[at, pl.ds(row, CHUNK), :] = cosine.astype(jnp.bfloat16)
            ramps[at, pl.ds(SHARED + row, CHUNK), :] = sine.astype(jnp.bfloat16)
            if at + 1 < bins:
                cosine, sine = (
                    cosine * turn_cos - sine * turn_sin,
                    sine * turn_cos + cosine * turn_sin,
                )


def dft(real, imag):
    count = len(real)
    if count == 1:
        return real, imag
    er, ei = dft(real[0::2], imag[0::2])
    odr, odi = dft(real[1::2], imag[1::2])
    half = count // 2
    outs = [None] * count
    for k in range(half):
        if k == 0:
            tr, ti = odr[k], odi[k]
        elif 4 * k == count:
            tr, ti = odi[k], -odr[k]
        else:
            c, s = math.cos(2 * math.pi * k / count), math.sin(2 * math.pi * k / count)
            tr, ti = odr[k] * c + odi[k] * s, odi[k] * c - odr[k] * s
        outs[k] = (er[k] + tr, ei[k] + ti)
        outs[k + half] = (er[k] - tr, ei[k] - ti)
    return [o[0] for o in outs], [o[1] for o in outs]


def channelize(held, twiddle, first, slab):
    slabs, members, _, bins, _ = held.shape
    per = members // RADIX
    for src in range(per):
        lane = src * slabs + slab
        real, imag = [], []
        for n2 in range(RADIX):
            real.append(held[slab, n2 * per + src, 0].astype(jnp.float32))
            imag.append(held[slab, n2 * per + src, 1].astype(jnp.float32))
        real, imag = dft(real, imag)
        cols = slice(lane * 128, lane * 128 + 128)
        cols_imag = slice(INNER + lane * 128, INNER + lane * 128 + 128)
        for k2 in range(RADIX):
            c, s = twiddle[0, k2 : k2 + 1, cols], twiddle[1, k2 : k2 + 1, cols]
            rows = slice(k2 * bins, k2 * bins + bins)
            first[rows, cols] = real[k2] * c - imag[k2] * s
            first[rows, cols_imag] = real[k2] * s + imag[k2] * c


def fill_matches(matches, units):
    rows, lanes = units.shape
    ids = lax.broadcasted_iota(jnp.int32, (rows, SHARED), 1) + 1
    for k2 in range(RADIX):
        for at in range(lanes // RADIX):
            lane = at * RADIX + k2
            same = (units[:, lane : lane + 1] == ids).astype(jnp.float32)
            matches[k2, at * rows : (at + 1) * rows, :] = same.astype(jnp.bfloat16)


def group_units(spectra, matches, bins):
    grouped = jnp.zeros((2 * bins, SHARED), jnp.float32)
    whole = jnp.zeros((2 * bins, INNER), jnp.float32)
    for k2 in range(RADIX):
        part = spectra[k2 * bins : (k2 + 1) * bins]
        part = jnp.concatenate([part[:, :INNER], part[:, INNER:]], 0)
        part = part.astype(jnp.bfloat16)
        whole += part.astype(jnp.float32)
        grouped += jnp.dot(part, matches[k2], preferred_element_type=jnp.float32)
    rest = jnp.sum(whole, 1, keepdims=True) - jnp.sum(grouped, 1, keepdims=True)
    return grouped, rest


def partner_order(members):
    return sorted(range(1, members), key=lambda o: -abs(o - members // 2))


def kernel(
    members, segments,
    raw, time_hbm, channel_hbm, filter_taps, units, dms, tap, twiddle,
    out,
    own, time, channel, later, tail, padded, spec, gain, extra, outgoing, held,
    ramps, matches, first, power_out, power_in,
    local_sem, halo_send, halo_recv, seg_send, seg_recv, pow_send, pow_recv,
):
    me = lax.axis_index("freq")
    seg = lax.axis_index("tm")
    own_len, width = own.shape
    bins = BINS // members
    kept = DMS // members
    loads = [
        pltpu.make_async_copy(raw, own, local_sem.at[0]),
        pltpu.make_async_copy(time_hbm, time, local_sem.at[1]),
        pltpu.make_async_copy(channel_hbm, channel, local_sem.at[2]),
    ]
    for load in loads[:2]:
        load.start()

    barrier = pltpu.get_barrier_semaphore()
    order = partner_order(members)
    for o in order:
        pl.semaphore_signal(
            barrier, inc=1, device_id={"freq": lax.rem(me + o, members)},
            device_id_type=pl.DeviceIdType.MESH,
        )

    @pl.when(seg > 0)
    def _():
        pl.semaphore_signal(
            barrier, inc=1, device_id={"tm": seg - 1}, device_id_type=pl.DeviceIdType.MESH
        )

    @pl.when(seg < segments - 1)
    def _():
        pl.semaphore_signal(
            barrier, inc=1, device_id={"tm": seg + 1}, device_id_type=pl.DeviceIdType.MESH
        )

    pl.semaphore_wait(
        barrier, members - 1 + jnp.minimum(seg, 1) + jnp.minimum(segments - 1 - seg, 1)
    )

    slabs = width // LANES

    def back_copy(slab):
        return pltpu.make_async_remote_copy(
            src_ref=raw.at[pl.ds(0, SHARED), pl.ds(slab * LANES, LANES)],
            dst_ref=later.at[slab],
            send_sem=halo_send.at[1 + slab], recv_sem=halo_recv.at[1 + slab],
            device_id={"tm": seg - 1}, device_id_type=pl.DeviceIdType.MESH,
        )

    def forward_copy():
        return pltpu.make_async_remote_copy(
            src_ref=raw.at[pl.ds(own_len - TAPS, TAPS)], dst_ref=tail,
            send_sem=halo_send.at[0], recv_sem=halo_recv.at[0],
            device_id={"tm": seg + 1}, device_id_type=pl.DeviceIdType.MESH,
        )

    @pl.when(seg > 0)
    def _():
        for slab in range(slabs):
            back_copy(slab).start()

    @pl.when(seg == 0)
    def _():
        tail[...] = jnp.zeros_like(tail)

    @pl.when(seg < segments - 1)
    def _():
        forward_copy().start()

    @pl.when(seg == segments - 1)
    def _():
        later[...] = jnp.zeros_like(later)

    loads[2].start()
    taps = filter_taps[...].astype(jnp.float32)
    padded[0:TAPS, :] = taps
    padded[TAPS:, :] = jnp.zeros_like(taps)
    gain[...] = jnp.dot(
        tap[...], taps, precision=lax.Precision.HIGHEST, preferred_element_type=jnp.float32
    )
    for load in loads[:2]:
        load.wait()
    spec[...] = jnp.dot(
        time[:, 0:own_len], own[...], preferred_element_type=jnp.float32
    )

    @pl.when(seg > 0)
    def _():
        forward_copy().wait_recv()

    def seg_copy(slab, slot, target):
        return pltpu.make_async_remote_copy(
            src_ref=outgoing.at[slab, target], dst_ref=held.at[slab, slot],
            send_sem=seg_send.at[slab, target], recv_sem=seg_recv.at[slab, slot],
            device_id={"freq": target}, device_id_type=pl.DeviceIdType.MESH,
        )

    def block(target, cols):
        row = pl.multiple_of(target * bins, bins)
        up, low = pl.ds(row, bins), pl.ds(BINS + row, bins)
        sr, si, gr, gi = spec[up, cols], spec[low, cols], gain[up, cols], gain[low, cols]
        real = sr * gr - si * gi + extra[up, :]
        imag = sr * gi + si * gr + extra[low, :]
        return real.astype(jnp.bfloat16), imag.astype(jnp.bfloat16)

    steps = SHARED // CHUNK // slabs
    for slab in range(slabs):
        cols = slice(slab * LANES, (slab + 1) * LANES)

        @pl.when(seg < segments - 1)
        def _():
            back_copy(slab).wait_recv()

        edge = tail[:, cols].astype(jnp.float32)
        edge = edge - later[slab, SHARED - TAPS :, :].astype(jnp.float32)
        fringe = jnp.zeros_like(edge)
        for e in range(1, TAPS):
            fringe = fringe + padded[e : e + TAPS, cols] * edge[TAPS - e : TAPS - e + 1]
        extra[...] = jnp.dot(
            tap[...], fringe * (1.0 / math.sqrt(DFT_LEN)),
            precision=lax.Precision.HIGHEST, preferred_element_type=jnp.float32,
        )
        spec[:, cols] += jnp.dot(
            time[:, own_len:], later[slab], preferred_element_type=jnp.float32
        )
        for o in order:
            target = lax.rem(me + o, members)
            outgoing[slab, target, 0], outgoing[slab, target, 1] = block(target, cols)
            seg_copy(slab, me, target).start()
        held[slab, me, 0], held[slab, me, 1] = block(me, cols)
        fill_ramps(ramps, dms, me * bins, slab * steps, (slab + 1) * steps)
    fill_matches(matches, units)

    for slab in range(slabs):
        for o in order:
            source = lax.rem(me + o, members)
            seg_copy(slab, source, source).wait_recv()
        channelize(held, twiddle, first, slab)
    loads[2].wait()
    spectra = jnp.dot(
        first[...].astype(jnp.bfloat16), channel[...], preferred_element_type=jnp.float32
    )
    grouped, rest = group_units(spectra, matches, bins)
    real, imag = grouped[:bins], grouped[bins:]
    upper = jnp.concatenate([real, -imag], 1)
    lower = jnp.concatenate([imag, real], 1)
    rows = []
    for at in range(bins):
        left = jnp.concatenate([upper[at : at + 1], lower[at : at + 1]], 0)
        total = jnp.dot(
            left.astype(jnp.bfloat16), ramps[at], preferred_element_type=jnp.float32
        )
        re = total[0:1] + rest[at : at + 1]
        im = total[1:2] + rest[bins + at : bins + at + 1]
        rows.append((re * re + im * im) * (1.0 / CHANNELS))
    turned = jnp.concatenate(rows, 0).T
    for target in range(members):
        power_out[target] = turned[target * kept : (target + 1) * kept]

    def power_copy(slot, target):
        return pltpu.make_async_remote_copy(
            src_ref=power_out.at[target], dst_ref=power_in.at[slot],
            send_sem=pow_send.at[target], recv_sem=pow_recv.at[slot],
            device_id={"freq": target}, device_id_type=pl.DeviceIdType.MESH,
        )

    for o in order:
        power_copy(me, lax.rem(me + o, members)).start()
    power_in[me] = power_out[me]
    for o in order:
        target = lax.rem(me + o, members)
        power_copy(target, target).wait_recv()
    out[...] = jnp.concatenate([power_in[source] for source in range(members)], 1)
    for o in order:
        target = lax.rem(me + o, members)
        for slab in range(slabs):
            seg_copy(slab, target, target).wait_send()
        power_copy(target, target).wait_send()

    @pl.when(seg > 0)
    def _():
        for slab in range(slabs):
            back_copy(slab).wait_send()

    @pl.when(seg < segments - 1)
    def _():
        forward_copy().wait_send()


def body(raw_samples, filter_taps, dm_trials, channel_units):
    members = lax.axis_size("freq")
    own_len, width = raw_samples.shape
    bins, kept, slabs = BINS // members, DMS // members, width // LANES
    time, tap, twiddle, channel = tables()
    units = channel_units.reshape(CHANNELS // LANES, LANES)
    vmem = pl.BlockSpec(memory_space=pltpu.VMEM)
    anywhere = pl.BlockSpec(memory_space=pl.ANY)
    dma = pltpu.SemaphoreType.DMA
    power = pl.pallas_call(
        functools.partial(kernel, members, lax.axis_size("tm")),
        out_shape=jax.ShapeDtypeStruct((kept, BINS), jnp.float32),
        in_specs=[anywhere] * 3 + [vmem] * 5,
        out_specs=vmem,
        scratch_shapes=[
            pltpu.VMEM((own_len, width), jnp.bfloat16),
            pltpu.VMEM(time.shape, jnp.bfloat16),
            pltpu.VMEM(channel.shape, jnp.bfloat16),
            pltpu.VMEM((width // LANES, SHARED, LANES), jnp.bfloat16),
            pltpu.VMEM((TAPS, width), jnp.bfloat16),
            pltpu.VMEM((2 * TAPS, width), jnp.float32),
            pltpu.VMEM((2 * BINS, width), jnp.float32),
            pltpu.VMEM((2 * BINS, width), jnp.float32),
            pltpu.VMEM((2 * BINS, LANES), jnp.float32),
            pltpu.VMEM((slabs, members, 2, bins, LANES), jnp.bfloat16),
            pltpu.VMEM((slabs, members, 2, bins, LANES), jnp.bfloat16),
            pltpu.VMEM((bins, 2 * SHARED, DMS), jnp.bfloat16),
            pltpu.VMEM((RADIX, INNER, SHARED), jnp.bfloat16),
            pltpu.VMEM((RADIX * bins, 2 * INNER), jnp.float32),
            pltpu.VMEM((members, kept, bins), jnp.float32),
            pltpu.VMEM((members, kept, bins), jnp.float32),
            dma((3,)), dma((1 + slabs,)), dma((1 + slabs,)),
            dma((slabs, members)), dma((slabs, members)), dma((members,)), dma((members,)),
        ],
        compiler_params=pltpu.CompilerParams(
            vmem_limit_bytes=56 * 2**20, collective_id=0, has_side_effects=True
        ),
    )(raw_samples, time, channel, filter_taps, units, dm_trials.reshape(1, DMS), tap, twiddle)
    return power[None]


def solution(mesh):
    in_specs = (P(("beam", "tm"), "freq"), P(None, "freq"), P(), P())
    out_specs = P(("beam", "tm"), "freq", None)
    return jax.shard_map(body, mesh=mesh, in_specs=in_specs, out_specs=out_specs, check_vma=False)
```

profile of v0, /device:TPU:0, one launch (start us, length us, event | category | flops | bytes accessed | tf_op | source)
XLA Modules:
  0.0 36.1 jit_solution(15442145149471137446)
XLA Ops:
  0.0 34.7 %shard_map.82 = f32[32,256]{1,0:T(8,128)} custom-call(bf16[1536,512]{1,0:T(8,128)(2,1)} %raw.1, bf16[512,2048]{1,0:T(8,128)(2,1)} %constant.8.clone.time_hbm, bf16[1024,1024]{1,0:T(8,128)(2,1)} %constant.11.clone.channel_hbm, bf16[16,512]{1,0:T(8,128)(2,1)} %filter_taps.1, s32[32,128]{1,0:T(8,128)} %bitcast.4, s32[1,256]{1,0:T(1,128)} %bitcast.5, ...), custom_call_target="tpu_custom_call" | custom-call | tf_op jit(solution)/shard_map/pallas_call | solution.py:356
  34.7 1.4 %copy.10 = f32[1,32,256]{2,1,0:T(8,128)} copy(f32[1,32,256]{2,1,0:T(8,128)} %bitcast.3) | data formatting | bytes 65536
where the time goes:
time: 36.3 us; the launch traced here: 36.1 us
  Pallas kernels  34.7 us (96%)
  local copies, waits for them, and re-layouts  1.38 us (4%)
    pallas_call x1, Pallas kernels, body(): pl.pallas_call(functools.partial(kernel, members, lax.axis_size('tm')), o...  34.7 us
    unnamed x1, local copies, waits for them, and re-layouts  1.38 us

commit v1 on v0

--- a/solution.py
+++ b/solution.py
@@ -355,7 +355,7 @@
     dma = pltpu.SemaphoreType.DMA
     power = pl.pallas_call(
         functools.partial(kernel, members, lax.axis_size("tm")),
-        out_shape=jax.ShapeDtypeStruct((kept, BINS), jnp.float32),
+        out_shape=pltpu.VMEM((kept, BINS), jnp.float32),
         in_specs=[anywhere] * 3 + [vmem] * 5,
         out_specs=vmem,
         scratch_shapes=[

time: 36.3 us -> 34.9 us (0.961)
  local copies, waits for them, and re-layouts: 1.38 us -> 0.62 us
  Pallas kernels: 34.7 us -> 34.1 us
    unnamed x1, local copies, waits for them, and re-layouts: 1.38 us -> 0.62 us
    pallas_call x1, Pallas kernels: 34.7 us -> 34.1 us  [body(): pl.pallas_call(functools.partial(kernel, members, lax.axis_size('tm')), o...]
where the time goes in v1:
time: 34.9 us; the launch traced here: 34.7 us
  Pallas kernels  34.1 us (98%)
  local copies, waits for them, and re-layouts  0.62 us (2%)
    pallas_call x1, Pallas kernels, body(): pl.pallas_call(functools.partial(kernel, members, lax.axis_size('tm')), o...  34.1 us

profile of v1, /device:TPU:0, one launch (start us, length us, event | category | flops | bytes accessed | tf_op | source)
XLA Modules:
  0.0 34.7 jit_solution(6151836533072644741)
XLA Ops:
  0.0 34.1 %shard_map.82 = f32[32,256]{1,0:T(8,128)S(1)} custom-call(bf16[1536,512]{1,0:T(8,128)(2,1)} %raw.1, bf16[512,2048]{1,0:T(8,128)(2,1)} %constant.8.clone.time_hbm, bf16[1024,1024]{1,0:T(8,128)(2,1)} %constant.11.clone.channel_hbm, bf16[16,512]{1,0:T(8,128)(2,1)} %filter_taps.1, s32[32,128]{1,0:T(8,128)} %bitcast.4, s32[1,256]{1,0:T(1,128)} %bitcast.5, ...), custom_call_target="tpu_custom_call" | custom-call | tf_op jit(solution)/shard_map/pallas_call | solution.py:356
  34.1 0.6 %copy.10 = f32[1,32,256]{2,1,0:T(8,128)} copy(f32[1,32,256]{2,1,0:T(8,128)S(1)} %bitcast.3) | data formatting | bytes 65536

commit v2 on v1

--- a/solution.py
+++ b/solution.py
@@ -20,14 +20,68 @@
 INNER = CHANNELS // RADIX
 CHUNK = 16
 LANES = 128
+SLAB = 256
+KEPT = 160
+
+
+def band_basis():
+    at = np.arange(SHARED)
+    diag = ((SHARED - 1) / 2 - at) ** 2 * math.cos(2 * math.pi * BINS / DFT_LEN)
+    off = at[1:] * (SHARED - at[1:]) / 2.0
+    square = off * off
+    low = np.full(KEPT, -float(SHARED * SHARED))
+    high = np.full(KEPT, float(SHARED * SHARED))
+    wanted = SHARED - np.arange(KEPT)
+    for _ in range(70):
+        middle = (low + high) / 2
+        pivot = diag[0] - middle
+        below = (pivot < 0).astype(np.int64)
+        for row in range(1, SHARED):
+            pivot = np.where(pivot == 0, 1e-30, pivot)
+            pivot = diag[row] - middle - square[row - 1] / pivot
+            below += pivot < 0
+        high = np.where(below >= wanted, middle, high)
+        low = np.where(below >= wanted, low, middle)
+    value = (low + high) / 2
+    down, up = np.zeros((SHARED, KEPT)), np.zeros((SHARED, KEPT))
+    down[0], up[-1] = diag[0] - value, diag[-1] - value
+    for row in range(1, SHARED):
+        down[row] = diag[row] - value - square[row - 1] / down[row - 1]
+        back = SHARED - 1 - row
+        up[back] = diag[back] - value - square[back] / up[back + 1]
+    twist = np.argmin(np.abs(down + up - (diag[:, None] - value)), 0)
+    basis = np.zeros((SHARED, KEPT))
+    basis[twist, np.arange(KEPT)] = 1.0
+    for row in range(1, SHARED):
+        basis[row] = np.where(row > twist, -off[row - 1] * basis[row - 1] / up[row], basis[row])
+        back = SHARED - 1 - row
+        step = -off[back] * basis[back + 1] / down[back]
+        basis[back] = np.where(back < twist, step, basis[back])
+    total = np.zeros(KEPT)
+    for row in range(SHARED):
+        total = total + basis[row] * basis[row]
+    return (basis / np.sqrt(total)).T
+
+
+def split(values, count):
+    parts = []
+    for _ in range(count):
+        part = np.asarray(values).astype(jnp.bfloat16)
+        parts.append(part)
+        values = values - part.astype(np.float64)
+    return parts
 
 
 def tables():
     bins = np.arange(BINS)[:, None]
     angle = 2 * np.pi * (bins * np.arange(DFT_LEN)[None, :] % DFT_LEN) / DFT_LEN
     time = np.concatenate([np.cos(angle), -np.sin(angle)], 0) / math.sqrt(DFT_LEN)
+    basis = band_basis()
+    shrink = np.concatenate(split(basis, 2), 0)
+    grow = np.concatenate(split(np.dot(time[:, DFT_LEN - SHARED :], basis.T), 2), 1)
     angle = 2 * np.pi * (bins * np.arange(TAPS)[None, :]) / DFT_LEN
-    tap = np.concatenate([np.cos(angle), -np.sin(angle)], 0)
+    tap = split(np.concatenate([np.cos(angle), -np.sin(angle)], 0), 3)
+    tap = np.concatenate([tap[0], tap[1], tap[2], tap[0], tap[1], tap[0]], 1)
     ids = np.arange(INNER)
     angle = 2 * np.pi * (np.arange(RADIX)[:, None] * ids[None, :]) / CHANNELS
     twiddle = np.stack([np.cos(angle), -np.sin(angle)]) / math.sqrt(RADIX)
@@ -36,10 +90,12 @@
     cosine, sine = np.cos(angle), np.sin(angle)
     channel = np.block([[cosine, -sine], [sine, cosine]]) / math.sqrt(INNER)
     return (
-        jnp.asarray(time, jnp.bfloat16),
-        jnp.asarray(tap, jnp.float32),
+        jnp.asarray(time[:, : DFT_LEN - SHARED], jnp.bfloat16),
+        jnp.asarray(channel, jnp.bfloat16),
+        jnp.asarray(shrink),
+        jnp.asarray(grow),
+        jnp.asarray(tap),
         jnp.asarray(twiddle, jnp.float32),
-        jnp.asarray(channel, jnp.bfloat16),
     )
 
 
@@ -104,7 +160,7 @@
 
 
 def channelize(held, twiddle, first, slab):
-    slabs, members, _, bins, _ = held.shape
+    slabs, members, _, bins, wide = held.shape
     per = members // RADIX
     for src in range(per):
         lane = src * slabs + slab
@@ -113,8 +169,8 @@
             real.append(held[slab, n2 * per + src, 0].astype(jnp.float32))
             imag.append(held[slab, n2 * per + src, 1].astype(jnp.float32))
         real, imag = dft(real, imag)
-        cols = slice(lane * 128, lane * 128 + 128)
-        cols_imag = slice(INNER + lane * 128, INNER + lane * 128 + 128)
+        cols = slice(lane * wide, lane * wide + wide)
+        cols_imag = slice(INNER + lane * wide, INNER + lane * wide + wide)
         for k2 in range(RADIX):
             c, s = twiddle[0, k2 : k2 + 1, cols], twiddle[1, k2 : k2 + 1, cols]
             rows = slice(k2 * bins, k2 * bins + bins)
@@ -151,10 +207,10 @@
 
 def kernel(
     members, segments,
-    raw, time_hbm, channel_hbm, filter_taps, units, dms, tap, twiddle,
+    raw, time_hbm, channel_hbm, shrink_hbm, grow_hbm, filter_taps, units, dms, tap, twiddle,
     out,
-    own, time, channel, later, tail, padded, spec, gain, extra, outgoing, held,
-    ramps, matches, first, power_out, power_in,
+    own, time, channel, shrink, grow, edges, later, tail, padded, spec, gain, extra,
+    outgoing, held, ramps, matches, first, power_out, power_in,
     local_sem, halo_send, halo_recv, seg_send, seg_recv, pow_send, pow_recv,
 ):
     me = lax.axis_index("freq")
@@ -162,12 +218,17 @@
     own_len, width = own.shape
     bins = BINS // members
     kept = DMS // members
+    slabs, _, wide = later.shape
+    head, rest = pl.ds(0, SHARED), pl.ds(SHARED, own_len - SHARED)
     loads = [
-        pltpu.make_async_copy(raw, own, local_sem.at[0]),
-        pltpu.make_async_copy(time_hbm, time, local_sem.at[1]),
-        pltpu.make_async_copy(channel_hbm, channel, local_sem.at[2]),
+        pltpu.make_async_copy(raw.at[head], own.at[head], local_sem.at[0]),
+        pltpu.make_async_copy(shrink_hbm, shrink, local_sem.at[1]),
+        pltpu.make_async_copy(raw.at[rest], own.at[rest], local_sem.at[2]),
+        pltpu.make_async_copy(time_hbm, time, local_sem.at[3]),
+        pltpu.make_async_copy(grow_hbm, grow, local_sem.at[4]),
+        pltpu.make_async_copy(channel_hbm, channel, local_sem.at[5]),
     ]
-    for load in loads[:2]:
+    for load in loads:
         load.start()
 
     barrier = pltpu.get_barrier_semaphore()
@@ -190,16 +251,25 @@
             barrier, inc=1, device_id={"tm": seg + 1}, device_id_type=pl.DeviceIdType.MESH
         )
 
+    for load in loads[:2]:
+        load.wait()
+
+    @pl.when(seg > 0)
+    def _():
+        both = jnp.dot(shrink[...], own[0:SHARED, :], preferred_element_type=jnp.float32)
+        both = (both[:KEPT] + both[KEPT:]).astype(jnp.bfloat16)
+        for slab in range(slabs):
+            cols = slice(slab * wide, (slab + 1) * wide)
+            edges[slab, 0:KEPT, :] = both[:, cols]
+            edges[slab, KEPT:, :] = own[SHARED - TAPS : SHARED, cols]
+
     pl.semaphore_wait(
         barrier, members - 1 + jnp.minimum(seg, 1) + jnp.minimum(segments - 1 - seg, 1)
     )
 
-    slabs = width // LANES
-
     def back_copy(slab):
         return pltpu.make_async_remote_copy(
-            src_ref=raw.at[pl.ds(0, SHARED), pl.ds(slab * LANES, LANES)],
-            dst_ref=later.at[slab],
+            src_ref=edges.at[slab], dst_ref=later.at[slab],
             send_sem=halo_send.at[1 + slab], recv_sem=halo_recv.at[1 + slab],
             device_id={"tm": seg - 1}, device_id_type=pl.DeviceIdType.MESH,
         )
@@ -228,18 +298,19 @@
     def _():
         later[...] = jnp.zeros_like(later)
 
-    loads[2].start()
-    taps = filter_taps[...].astype(jnp.float32)
-    padded[0:TAPS, :] = taps
-    padded[TAPS:, :] = jnp.zeros_like(taps)
+    taps = filter_taps[...]
+    padded[0:TAPS, :] = taps.astype(jnp.float32)
+    padded[TAPS:, :] = jnp.zeros((TAPS, width), jnp.float32)
     gain[...] = jnp.dot(
-        tap[...], taps, precision=lax.Precision.HIGHEST, preferred_element_type=jnp.float32
+        tap[:, 0 : 3 * TAPS], jnp.concatenate([taps] * 3, 0),
+        preferred_element_type=jnp.float32,
     )
-    for load in loads[:2]:
+    for load in loads[2:4]:
         load.wait()
-    spec[...] = jnp.dot(
-        time[:, 0:own_len], own[...], preferred_element_type=jnp.float32
-    )
+    spec[...] = jnp.dot(time[...], own[...], preferred_element_type=jnp.float32)
+    loads[4].wait()
+    fill_matches(matches, units)
+    fill_ramps(ramps, dms, me * bins, 0, 6)
 
     @pl.when(seg > 0)
     def _():
@@ -260,40 +331,46 @@
         imag = sr * gi + si * gr + extra[low, :]
         return real.astype(jnp.bfloat16), imag.astype(jnp.bfloat16)
 
-    steps = SHARED // CHUNK // slabs
     for slab in range(slabs):
-        cols = slice(slab * LANES, (slab + 1) * LANES)
+        cols = slice(slab * wide, (slab + 1) * wide)
 
         @pl.when(seg < segments - 1)
         def _():
             back_copy(slab).wait_recv()
 
         edge = tail[:, cols].astype(jnp.float32)
-        edge = edge - later[slab, SHARED - TAPS :, :].astype(jnp.float32)
+        edge = edge - later[slab, KEPT:, :].astype(jnp.float32)
         fringe = jnp.zeros_like(edge)
         for e in range(1, TAPS):
             fringe = fringe + padded[e : e + TAPS, cols] * edge[TAPS - e : TAPS - e + 1]
+        fringe = fringe * (1.0 / math.sqrt(DFT_LEN))
+        one = fringe.astype(jnp.bfloat16)
+        left = fringe - one.astype(jnp.float32)
+        two = left.astype(jnp.bfloat16)
+        three = (left - two.astype(jnp.float32)).astype(jnp.bfloat16)
         extra[...] = jnp.dot(
-            tap[...], fringe * (1.0 / math.sqrt(DFT_LEN)),
-            precision=lax.Precision.HIGHEST, preferred_element_type=jnp.float32,
+            tap[...], jnp.concatenate([one, one, one, two, two, three], 0),
+            preferred_element_type=jnp.float32,
         )
         spec[:, cols] += jnp.dot(
-            time[:, own_len:], later[slab], preferred_element_type=jnp.float32
+            grow[...], jnp.concatenate([later[slab, 0:KEPT, :]] * 2, 0),
+            preferred_element_type=jnp.float32,
         )
         for o in order:
             target = lax.rem(me + o, members)
             outgoing[slab, target, 0], outgoing[slab, target, 1] = block(target, cols)
             seg_copy(slab, me, target).start()
         held[slab, me, 0], held[slab, me, 1] = block(me, cols)
-        fill_ramps(ramps, dms, me * bins, slab * steps, (slab + 1) * steps)
-    fill_matches(matches, units)
+        if slab + 1 < slabs:
+            fill_ramps(ramps, dms, me * bins, 6, 10)
+    fill_ramps(ramps, dms, me * bins, 10 if slabs > 1 else 6, SHARED // CHUNK)
 
     for slab in range(slabs):
         for o in order:
             source = lax.rem(me + o, members)
             seg_copy(slab, source, source).wait_recv()
         channelize(held, twiddle, first, slab)
-    loads[2].wait()
+    loads[5].wait()
     spectra = jnp.dot(
         first[...].astype(jnp.bfloat16), channel[...], preferred_element_type=jnp.float32
     )
@@ -347,8 +424,9 @@
 def body(raw_samples, filter_taps, dm_trials, channel_units):
     members = lax.axis_size("freq")
     own_len, width = raw_samples.shape
-    bins, kept, slabs = BINS // members, DMS // members, width // LANES
-    time, tap, twiddle, channel = tables()
+    bins, kept, wide = BINS // members, DMS // members, min(SLAB, width)
+    slabs, rows = width // wide, KEPT + TAPS
+    time, channel, shrink, grow, tap, twiddle = tables()
     units = channel_units.reshape(CHANNELS // LANES, LANES)
     vmem = pl.BlockSpec(memory_space=pltpu.VMEM)
     anywhere = pl.BlockSpec(memory_space=pl.ANY)
@@ -356,32 +434,38 @@
     power = pl.pallas_call(
         functools.partial(kernel, members, lax.axis_size("tm")),
         out_shape=pltpu.VMEM((kept, BINS), jnp.float32),
-        in_specs=[anywhere] * 3 + [vmem] * 5,
+        in_specs=[anywhere] * 5 + [vmem] * 5,
         out_specs=vmem,
         scratch_shapes=[
             pltpu.VMEM((own_len, width), jnp.bfloat16),
             pltpu.VMEM(time.shape, jnp.bfloat16),
             pltpu.VMEM(channel.shape, jnp.bfloat16),
-            pltpu.VMEM((width // LANES, SHARED, LANES), jnp.bfloat16),
+            pltpu.VMEM(shrink.shape, jnp.bfloat16),
+            pltpu.VMEM(grow.shape, jnp.bfloat16),
+            pltpu.VMEM((slabs, rows, wide), jnp.bfloat16),
+            pltpu.VMEM((slabs, rows, wide), jnp.bfloat16),
             pltpu.VMEM((TAPS, width), jnp.bfloat16),
             pltpu.VMEM((2 * TAPS, width), jnp.float32),
             pltpu.VMEM((2 * BINS, width), jnp.float32),
             pltpu.VMEM((2 * BINS, width), jnp.float32),
-            pltpu.VMEM((2 * BINS, LANES), jnp.float32),
-            pltpu.VMEM((slabs, members, 2, bins, LANES), jnp.bfloat16),
-            pltpu.VMEM((slabs, members, 2, bins, LANES), jnp.bfloat16),
+            pltpu.VMEM((2 * BINS, wide), jnp.float32),
+            pltpu.VMEM((slabs, members, 2, bins, wide), jnp.bfloat16),
+            pltpu.VMEM((slabs, members, 2, bins, wide), jnp.bfloat16),
             pltpu.VMEM((bins, 2 * SHARED, DMS), jnp.bfloat16),
             pltpu.VMEM((RADIX, INNER, SHARED), jnp.bfloat16),
             pltpu.VMEM((RADIX * bins, 2 * INNER), jnp.float32),
             pltpu.VMEM((members, kept, bins), jnp.float32),
             pltpu.VMEM((members, kept, bins), jnp.float32),
-            dma((3,)), dma((1 + slabs,)), dma((1 + slabs,)),
+            dma((6,)), dma((1 + slabs,)), dma((1 + slabs,)),
             dma((slabs, members)), dma((slabs, members)), dma((members,)), dma((members,)),
         ],
         compiler_params=pltpu.CompilerParams(
             vmem_limit_bytes=56 * 2**20, collective_id=0, has_side_effects=True
         ),
-    )(raw_samples, time, channel, filter_taps, units, dm_trials.reshape(1, DMS), tap, twiddle)
+    )(
+        raw_samples, time, channel, shrink, grow,
+        filter_taps, units, dm_trials.reshape(1, DMS), tap, twiddle,
+    )
     return power[None]
 
 

time: 34.9 us -> 33.2 us (0.951)
  Pallas kernels: 34.1 us -> 32.4 us
    pallas_call x1, Pallas kernels: 34.1 us -> 32.4 us  [body(): pl.pallas_call(functools.partial(kernel, members, lax.axis_size('tm')), o...]
where the time goes in v2:
time: 33.2 us; the launch traced here: 33 us
  Pallas kernels  32.4 us (98%)
  local copies, waits for them, and re-layouts  0.62 us (2%)
    pallas_call x1, Pallas kernels, body(): pl.pallas_call(functools.partial(kernel, members, lax.axis_size('tm')), o...  32.4 us

profile of v2, /device:TPU:0, one launch (start us, length us, event | category | flops | bytes accessed | tf_op | source)
XLA Modules:
  0.0 33.0 jit_solution(15453022926318440774)
XLA Ops:
  0.0 32.4 %shard_map.100 = f32[32,256]{1,0:T(8,128)S(1)} custom-call(bf16[1536,512]{1,0:T(8,128)(2,1)} %raw.1, bf16[512,1536]{1,0:T(8,128)(2,1)} %constant.12.clone.time_hbm, bf16[1024,1024]{1,0:T(8,128)(2,1)} %constant.13.clone.channel_hbm, bf16[320,512]{1,0:T(8,128)(2,1)} %constant.14.clone.shrink_hbm, bf16[512,320]{1,0:T(8,128)(2,1)} %constant.15.clone.grow_hbm, ...), custom_call_target="tpu_custom_call" | custom-call | tf_op jit(solution)/shard_map/pallas_call | solution.py:434
  32.4 0.6 %copy.12 = f32[1,32,256]{2,1,0:T(8,128)} copy(f32[1,32,256]{2,1,0:T(8,128)S(1)} %bitcast.3) | data formatting | bytes 65536

commit v3 on v2

--- a/solution.py
+++ b/solution.py
@@ -16,7 +16,7 @@
 DMS = 256
 DM_STEPS = 1024
 CHANNELS = 4096
-RADIX = 8
+RADIX = 16
 INNER = CHANNELS // RADIX
 CHUNK = 16
 LANES = 128
@@ -72,7 +72,7 @@
     return parts
 
 
-def tables():
+def tables(chips):
     bins = np.arange(BINS)[:, None]
     angle = 2 * np.pi * (bins * np.arange(DFT_LEN)[None, :] % DFT_LEN) / DFT_LEN
     time = np.concatenate([np.cos(angle), -np.sin(angle)], 0) / math.sqrt(DFT_LEN)
@@ -83,8 +83,10 @@
     tap = split(np.concatenate([np.cos(angle), -np.sin(angle)], 0), 3)
     tap = np.concatenate([tap[0], tap[1], tap[2], tap[0], tap[1], tap[0]], 1)
     ids = np.arange(INNER)
-    angle = 2 * np.pi * (np.arange(RADIX)[:, None] * ids[None, :]) / CHANNELS
-    twiddle = np.stack([np.cos(angle), -np.sin(angle)]) / math.sqrt(RADIX)
+    start = (np.arange(chips) * (CHANNELS // chips))[:, None, None]
+    angle = np.arange(RADIX)[:, None] * (ids[None, :] + start) % CHANNELS
+    angle = 2 * np.pi * angle / CHANNELS
+    twiddle = np.stack([np.cos(angle), -np.sin(angle)], 1) / math.sqrt(RADIX)
     spread = ids.reshape(CHANNELS // LANES, LANES // RADIX).T.reshape(-1)
     angle = 2 * np.pi * (ids[:, None] * spread[None, :] % INNER) / INNER
     cosine, sine = np.cos(angle), np.sin(angle)
@@ -159,23 +161,35 @@
     return [o[0] for o in outs], [o[1] for o in outs]
 
 
-def channelize(held, twiddle, first, slab):
-    slabs, members, _, bins, wide = held.shape
-    per = members // RADIX
-    for src in range(per):
-        lane = src * slabs + slab
-        real, imag = [], []
-        for n2 in range(RADIX):
-            real.append(held[slab, n2 * per + src, 0].astype(jnp.float32))
-            imag.append(held[slab, n2 * per + src, 1].astype(jnp.float32))
-        real, imag = dft(real, imag)
-        cols = slice(lane * wide, lane * wide + wide)
-        cols_imag = slice(INNER + lane * wide, INNER + lane * wide + wide)
-        for k2 in range(RADIX):
-            c, s = twiddle[0, k2 : k2 + 1, cols], twiddle[1, k2 : k2 + 1, cols]
+def channelize(pair, twiddle, first, chip):
+    cores, slabs, _, _, bins, wide = pair.shape
+    real, imag = [], []
+    for core in range(cores):
+        for slab in range(slabs):
+            real.append(pair[core, slab, 0, chip].astype(jnp.float32))
+            imag.append(pair[core, slab, 1, chip].astype(jnp.float32))
+    join = max(1, INNER // wide)
+    real = [jnp.concatenate(real[at : at + join], 1) for at in range(0, len(real), join)]
+    imag = [jnp.concatenate(imag[at : at + join], 1) for at in range(0, len(imag), join)]
+    fold = len(real)
+    stride = RADIX // fold
+    for r in range(stride):
+        turned_real, turned_imag = [], []
+        for f in range(fold):
+            c, s = math.cos(2 * math.pi * r * f / RADIX), math.sin(2 * math.pi * r * f / RADIX)
+            if r * f == 0:
+                turned_real.append(real[f])
+                turned_imag.append(imag[f])
+            else:
+                turned_real.append(real[f] * c + imag[f] * s)
+                turned_imag.append(imag[f] * c - real[f] * s)
+        outs_real, outs_imag = dft(turned_real, turned_imag)
+        for at in range(fold):
+            k2 = r + stride * at
+            c, s = twiddle[0, k2 : k2 + 1, :], twiddle[1, k2 : k2 + 1, :]
             rows = slice(k2 * bins, k2 * bins + bins)
-            first[rows, cols] = real[k2] * c - imag[k2] * s
-            first[rows, cols_imag] = real[k2] * s + imag[k2] * c
+            first[rows, 0:INNER] = outs_real[at] * c - outs_imag[at] * s
+            first[rows, INNER:] = outs_real[at] * s + outs_imag[at] * c
 
 
 def fill_matches(matches, units):
@@ -207,14 +221,18 @@
 
 def kernel(
     members, segments,
-    raw, time_hbm, channel_hbm, shrink_hbm, grow_hbm, filter_taps, units, dms, tap, twiddle,
+    raw, time_hbm, channel_hbm, shrink_hbm, grow_hbm, twiddle_hbm,
+    filter_taps, units, dms, tap,
     out,
-    own, time, channel, shrink, grow, edges, later, tail, padded, spec, gain, extra,
-    outgoing, held, ramps, matches, first, power_out, power_in,
-    local_sem, halo_send, halo_recv, seg_send, seg_recv, pow_send, pow_recv,
+    own, time, channel, shrink, grow, twiddle, edges, later, tail, padded, spec, gain, extra,
+    halves, pair, ramps, matches, first, sums_out, sums_in, power_out, power_in,
+    local_sem, halo_send, halo_recv, pair_send, pair_recv, sum_send, sum_recv,
+    pow_send, pow_recv,
 ):
     me = lax.axis_index("freq")
     seg = lax.axis_index("tm")
+    chips = members // 2
+    chip, core = me // 2, me % 2
     own_len, width = own.shape
     bins = BINS // members
     kept = DMS // members
@@ -227,6 +245,7 @@
         pltpu.make_async_copy(time_hbm, time, local_sem.at[3]),
         pltpu.make_async_copy(grow_hbm, grow, local_sem.at[4]),
         pltpu.make_async_copy(channel_hbm, channel, local_sem.at[5]),
+        pltpu.make_async_copy(twiddle_hbm.at[chip], twiddle, local_sem.at[6]),
     ]
     for load in loads:
         load.start()
@@ -310,21 +329,22 @@
     spec[...] = jnp.dot(time[...], own[...], preferred_element_type=jnp.float32)
     loads[4].wait()
     fill_matches(matches, units)
-    fill_ramps(ramps, dms, me * bins, 0, 6)
+    first_bin = core * (BINS // 2) + chip * bins
+    fill_ramps(ramps, dms, first_bin, 0, 8)
 
     @pl.when(seg > 0)
     def _():
         forward_copy().wait_recv()
 
-    def seg_copy(slab, slot, target):
+    def pair_copy(slab):
         return pltpu.make_async_remote_copy(
-            src_ref=outgoing.at[slab, target], dst_ref=held.at[slab, slot],
-            send_sem=seg_send.at[slab, target], recv_sem=seg_recv.at[slab, slot],
-            device_id={"freq": target}, device_id_type=pl.DeviceIdType.MESH,
-        )
-
-    def block(target, cols):
-        row = pl.multiple_of(target * bins, bins)
+            src_ref=halves.at[slab], dst_ref=pair.at[core, slab],
+            send_sem=pair_send.at[slab], recv_sem=pair_recv.at[slab],
+            device_id={"freq": me + 1 - 2 * core}, device_id_type=pl.DeviceIdType.MESH,
+        )
+
+    def block(half, at, cols):
+        row = pl.multiple_of(half * (BINS // 2) + at * bins, bins)
         up, low = pl.ds(row, bins), pl.ds(BINS + row, bins)
         sr, si, gr, gi = spec[up, cols], spec[low, cols], gain[up, cols], gain[low, cols]
         real = sr * gr - si * gi + extra[up, :]
@@ -356,25 +376,56 @@
             grow[...], jnp.concatenate([later[slab, 0:KEPT, :]] * 2, 0),
             preferred_element_type=jnp.float32,
         )
-        for o in order:
-            target = lax.rem(me + o, members)
-            outgoing[slab, target, 0], outgoing[slab, target, 1] = block(target, cols)
-            seg_copy(slab, me, target).start()
-        held[slab, me, 0], held[slab, me, 1] = block(me, cols)
-        if slab + 1 < slabs:
-            fill_ramps(ramps, dms, me * bins, 6, 10)
-    fill_ramps(ramps, dms, me * bins, 10 if slabs > 1 else 6, SHARED // CHUNK)
-
+        for at in range(chips):
+            halves[slab, 0, at], halves[slab, 1, at] = block(1 - core, at, cols)
+        pair_copy(slab).start()
+        for at in range(chips):
+            pair[core, slab, 0, at], pair[core, slab, 1, at] = block(core, at, cols)
+    fill_ramps(ramps, dms, first_bin, 8, 12)
+    for load in loads[5:]:
+        load.wait()
     for slab in range(slabs):
-        for o in order:
-            source = lax.rem(me + o, members)
-            seg_copy(slab, source, source).wait_recv()
-        channelize(held, twiddle, first, slab)
-    loads[5].wait()
-    spectra = jnp.dot(
-        first[...].astype(jnp.bfloat16), channel[...], preferred_element_type=jnp.float32
-    )
-    grouped, rest = group_units(spectra, matches, bins)
+        pair_copy(slab).wait_recv()
+
+    def sum_copy(slot, target):
+        return pltpu.make_async_remote_copy(
+            src_ref=sums_out.at[target], dst_ref=sums_in.at[slot],
+            send_sem=sum_send.at[target], recv_sem=sum_recv.at[slot],
+            device_id={"freq": 2 * target + core}, device_id_type=pl.DeviceIdType.MESH,
+        )
+
+    def partial(at):
+        channelize(pair, twiddle, first, at)
+        spectra = jnp.dot(
+            first[...].astype(jnp.bfloat16), channel[...], preferred_element_type=jnp.float32
+        )
+        return group_units(spectra, matches, bins)
+
+    ones = lax.broadcasted_iota(jnp.int32, (2 * bins, LANES), 0)
+    ones = (ones == lax.broadcasted_iota(jnp.int32, (2 * bins, LANES), 1)).astype(jnp.float32)
+    blocks = SHARED // LANES
+    hops = partner_order(chips)[::-1]
+    for o in hops:
+        target = lax.rem(chip + o, chips)
+        grouped, rest = partial(target)
+        line = jnp.sum(rest * ones, 0, keepdims=True)
+        high = line.astype(jnp.bfloat16).astype(jnp.float32)
+        row = lax.broadcasted_iota(jnp.int32, (TAPS, LANES), 0)
+        lines = jnp.where(row == 0, high, jnp.where(row == 1, line - high, 0.0))
+        pieces = [grouped[:, at * LANES : (at + 1) * LANES] for at in range(blocks)]
+        sums_out[target] = jnp.concatenate(pieces + [lines], 0).astype(jnp.bfloat16)
+        sum_copy(chip, target).start()
+    grouped, rest = partial(chip)
+    fill_ramps(ramps, dms, first_bin, 12, SHARED // CHUNK)
+    for o in hops:
+        source = lax.rem(chip + o, chips)
+        sum_copy(source, source).wait_recv()
+        came = sums_in[source].astype(jnp.float32)
+        size = 2 * bins
+        pieces = [came[at * size : (at + 1) * size] for at in range(blocks)]
+        grouped += jnp.concatenate(pieces, 1)
+        line = came[blocks * size : blocks * size + 1] + came[blocks * size + 1 : blocks * size + 2]
+        rest += jnp.sum(line * ones, 1, keepdims=True)
     real, imag = grouped[:bins], grouped[bins:]
     upper = jnp.concatenate([real, -imag], 1)
     lower = jnp.concatenate([imag, real], 1)
@@ -404,12 +455,16 @@
     for o in order:
         target = lax.rem(me + o, members)
         power_copy(target, target).wait_recv()
-    out[...] = jnp.concatenate([power_in[source] for source in range(members)], 1)
+    sources = [2 * at + half for half in range(2) for at in range(chips)]
+    out[...] = jnp.concatenate([power_in[source] for source in sources], 1)
     for o in order:
         target = lax.rem(me + o, members)
-        for slab in range(slabs):
-            seg_copy(slab, target, target).wait_send()
         power_copy(target, target).wait_send()
+    for slab in range(slabs):
+        pair_copy(slab).wait_send()
+    for o in hops:
+        target = lax.rem(chip + o, chips)
+        sum_copy(target, target).wait_send()
 
     @pl.when(seg > 0)
     def _():
@@ -426,7 +481,9 @@
     own_len, width = raw_samples.shape
     bins, kept, wide = BINS // members, DMS // members, min(SLAB, width)
     slabs, rows = width // wide, KEPT + TAPS
-    time, channel, shrink, grow, tap, twiddle = tables()
+    swap = 2 * bins * (SHARED // LANES) + TAPS
+    chips = members // 2
+    time, channel, shrink, grow, tap, twiddle = tables(chips)
     units = channel_units.reshape(CHANNELS // LANES, LANES)
     vmem = pl.BlockSpec(memory_space=pltpu.VMEM)
     anywhere = pl.BlockSpec(memory_space=pl.ANY)
@@ -434,7 +491,7 @@
     power = pl.pallas_call(
         functools.partial(kernel, members, lax.axis_size("tm")),
         out_shape=pltpu.VMEM((kept, BINS), jnp.float32),
-        in_specs=[anywhere] * 5 + [vmem] * 5,
+        in_specs=[anywhere] * 6 + [vmem] * 4,
         out_specs=vmem,
         scratch_shapes=[
             pltpu.VMEM((own_len, width), jnp.bfloat16),
@@ -442,6 +499,7 @@
             pltpu.VMEM(channel.shape, jnp.bfloat16),
             pltpu.VMEM(shrink.shape, jnp.bfloat16),
             pltpu.VMEM(grow.shape, jnp.bfloat16),
+            pltpu.VMEM(twiddle.shape[1:], jnp.float32),
             pltpu.VMEM((slabs, rows, wide), jnp.bfloat16),
             pltpu.VMEM((slabs, rows, wide), jnp.bfloat16),
             pltpu.VMEM((TAPS, width), jnp.bfloat16),
@@ -449,22 +507,24 @@
             pltpu.VMEM((2 * BINS, width), jnp.float32),
             pltpu.VMEM((2 * BINS, width), jnp.float32),
             pltpu.VMEM((2 * BINS, wide), jnp.float32),
-            pltpu.VMEM((slabs, members, 2, bins, wide), jnp.bfloat16),
-            pltpu.VMEM((slabs, members, 2, bins, wide), jnp.bfloat16),
+            pltpu.VMEM((slabs, 2, chips, bins, wide), jnp.bfloat16),
+            pltpu.VMEM((2, slabs, 2, chips, bins, wide), jnp.bfloat16),
             pltpu.VMEM((bins, 2 * SHARED, DMS), jnp.bfloat16),
             pltpu.VMEM((RADIX, INNER, SHARED), jnp.bfloat16),
             pltpu.VMEM((RADIX * bins, 2 * INNER), jnp.float32),
+            pltpu.VMEM((chips, swap, LANES), jnp.bfloat16),
+            pltpu.VMEM((chips, swap, LANES), jnp.bfloat16),
             pltpu.VMEM((members, kept, bins), jnp.float32),
             pltpu.VMEM((members, kept, bins), jnp.float32),
-            dma((6,)), dma((1 + slabs,)), dma((1 + slabs,)),
-            dma((slabs, members)), dma((slabs, members)), dma((members,)), dma((members,)),
+            dma((7,)), dma((1 + slabs,)), dma((1 + slabs,)), dma((slabs,)), dma((slabs,)),
+            dma((chips,)), dma((chips,)), dma((members,)), dma((members,)),
         ],
         compiler_params=pltpu.CompilerParams(
             vmem_limit_bytes=56 * 2**20, collective_id=0, has_side_effects=True
         ),
     )(
-        raw_samples, time, channel, shrink, grow,
-        filter_taps, units, dm_trials.reshape(1, DMS), tap, twiddle,
+        raw_samples, time, channel, shrink, grow, twiddle,
+        filter_taps, units, dm_trials.reshape(1, DMS), tap,
     )
     return power[None]
 

time: 33.2 us -> 32 us (0.964)
  Pallas kernels: 32.4 us -> 31.2 us
    pallas_call x1, Pallas kernels: 32.4 us -> 31.2 us  [body(): pl.pallas_call(functools.partial(kernel, members, lax.axis_size('tm')), o...]
where the time goes in v3:
time: 32 us; the launch traced here: 31.8 us
  Pallas kernels  31.2 us (98%)
  local copies, waits for them, and re-layouts  0.62 us (2%)
    pallas_call x1, Pallas kernels, body(): pl.pallas_call(functools.partial(kernel, members, lax.axis_size('tm')), o...  31.2 us

profile of v3, /device:TPU:0, one launch (start us, length us, event | category | flops | bytes accessed | tf_op | source)
XLA Modules:
  0.0 31.8 jit_solution(12678905298278841915)
XLA Ops:
  0.0 31.2 %shard_map.100 = f32[32,256]{1,0:T(8,128)S(1)} custom-call(bf16[1536,512]{1,0:T(8,128)(2,1)} %raw.1, bf16[512,1536]{1,0:T(8,128)(2,1)} %constant.12.clone.time_hbm, bf16[512,512]{1,0:T(8,128)(2,1)} %constant.13.clone.channel_hbm, bf16[320,512]{1,0:T(8,128)(2,1)} %constant.14.clone.shrink_hbm, bf16[512,320]{1,0:T(8,128)(2,1)} %constant.15.clone.grow_hbm, ...), custom_call_target="tpu_custom_call" | custom-call | tf_op jit(solution)/shard_map/pallas_call | solution.py:491
  31.2 0.6 %copy.12 = f32[1,32,256]{2,1,0:T(8,128)} copy(f32[1,32,256]{2,1,0:T(8,128)S(1)} %bitcast.3) | data formatting | bytes 65536

commit v4 on v3

--- a/solution.py
+++ b/solution.py
@@ -161,13 +161,14 @@
     return [o[0] for o in outs], [o[1] for o in outs]
 
 
-def channelize(pair, twiddle, first, chip):
-    cores, slabs, _, _, bins, wide = pair.shape
+def channelize(pair, twiddle, first, half):
+    cores, slabs, _, _, chips, size, wide = pair.shape
+    bins = chips * size
     real, imag = [], []
     for core in range(cores):
         for slab in range(slabs):
-            real.append(pair[core, slab, 0, chip].astype(jnp.float32))
-            imag.append(pair[core, slab, 1, chip].astype(jnp.float32))
+            real.append(pair[core, slab, half, 0].astype(jnp.float32).reshape(bins, wide))
+            imag.append(pair[core, slab, half, 1].astype(jnp.float32).reshape(bins, wide))
     join = max(1, INNER // wide)
     real = [jnp.concatenate(real[at : at + join], 1) for at in range(0, len(real), join)]
     imag = [jnp.concatenate(imag[at : at + join], 1) for at in range(0, len(imag), join)]
@@ -225,7 +226,8 @@
     filter_taps, units, dms, tap,
     out,
     own, time, channel, shrink, grow, twiddle, edges, later, tail, padded, spec, gain, extra,
-    halves, pair, ramps, matches, first, sums_out, sums_in, power_out, power_in,
+    halves, pair, ramps, matches, first, kept_sums, kept_rest, sums_out, sums_in,
+    power_out, power_in,
     local_sem, halo_send, halo_recv, pair_send, pair_recv, sum_send, sum_recv,
     pow_send, pow_recv,
 ):
@@ -330,22 +332,24 @@
     loads[4].wait()
     fill_matches(matches, units)
     first_bin = core * (BINS // 2) + chip * bins
-    fill_ramps(ramps, dms, first_bin, 0, 8)
+    fill_ramps(ramps, dms, first_bin, 0, 4)
 
     @pl.when(seg > 0)
     def _():
         forward_copy().wait_recv()
 
-    def pair_copy(slab):
+    _, _, parts, _, _, size, _ = pair.shape
+
+    def pair_copy(slab, part):
         return pltpu.make_async_remote_copy(
-            src_ref=halves.at[slab], dst_ref=pair.at[core, slab],
-            send_sem=pair_send.at[slab], recv_sem=pair_recv.at[slab],
+            src_ref=halves.at[slab, part], dst_ref=pair.at[core, slab, part],
+            send_sem=pair_send.at[slab, part], recv_sem=pair_recv.at[slab, part],
             device_id={"freq": me + 1 - 2 * core}, device_id_type=pl.DeviceIdType.MESH,
         )
 
-    def block(half, at, cols):
-        row = pl.multiple_of(half * (BINS // 2) + at * bins, bins)
-        up, low = pl.ds(row, bins), pl.ds(BINS + row, bins)
+    def block(half, part, at, cols):
+        row = pl.multiple_of(half * (BINS // 2) + at * bins + part * size, size)
+        up, low = pl.ds(row, size), pl.ds(BINS + row, size)
         sr, si, gr, gi = spec[up, cols], spec[low, cols], gain[up, cols], gain[low, cols]
         real = sr * gr - si * gi + extra[up, :]
         imag = sr * gi + si * gr + extra[low, :]
@@ -376,68 +380,81 @@
             grow[...], jnp.concatenate([later[slab, 0:KEPT, :]] * 2, 0),
             preferred_element_type=jnp.float32,
         )
-        for at in range(chips):
-            halves[slab, 0, at], halves[slab, 1, at] = block(1 - core, at, cols)
-        pair_copy(slab).start()
-        for at in range(chips):
-            pair[core, slab, 0, at], pair[core, slab, 1, at] = block(core, at, cols)
-    fill_ramps(ramps, dms, first_bin, 8, 12)
+        for part in range(parts):
+            for at in range(chips):
+                real, imag = block(1 - core, part, at, cols)
+                halves[slab, part, 0, at], halves[slab, part, 1, at] = real, imag
+            pair_copy(slab, part).start()
+        for part in range(parts):
+            for at in range(chips):
+                real, imag = block(core, part, at, cols)
+                pair[core, slab, part, 0, at], pair[core, slab, part, 1, at] = real, imag
+        if slab + 1 < slabs:
+            fill_ramps(ramps, dms, first_bin, 4, 8)
+    fill_ramps(ramps, dms, first_bin, 8 if slabs > 1 else 4, 10)
     for load in loads[5:]:
         load.wait()
-    for slab in range(slabs):
-        pair_copy(slab).wait_recv()
-
-    def sum_copy(slot, target):
+
+    def sum_copy(part, slot, target):
         return pltpu.make_async_remote_copy(
-            src_ref=sums_out.at[target], dst_ref=sums_in.at[slot],
-            send_sem=sum_send.at[target], recv_sem=sum_recv.at[slot],
+            src_ref=sums_out.at[part, target], dst_ref=sums_in.at[part, slot],
+            send_sem=sum_send.at[part, target], recv_sem=sum_recv.at[part, slot],
             device_id={"freq": 2 * target + core}, device_id_type=pl.DeviceIdType.MESH,
         )
 
-    def partial(at):
-        channelize(pair, twiddle, first, at)
+    ones = lax.broadcasted_iota(jnp.int32, (2 * size, LANES), 0)
+    ones = (ones == lax.broadcasted_iota(jnp.int32, (2 * size, LANES), 1)).astype(jnp.float32)
+    blocks = SHARED // LANES
+    hops = partner_order(chips)[::-1]
+    some = chips * size
+    for part in range(parts):
+        for slab in range(slabs):
+            pair_copy(slab, part).wait_recv()
+        channelize(pair, twiddle, first, part)
         spectra = jnp.dot(
             first[...].astype(jnp.bfloat16), channel[...], preferred_element_type=jnp.float32
         )
-        return group_units(spectra, matches, bins)
-
-    ones = lax.broadcasted_iota(jnp.int32, (2 * bins, LANES), 0)
-    ones = (ones == lax.broadcasted_iota(jnp.int32, (2 * bins, LANES), 1)).astype(jnp.float32)
-    blocks = SHARED // LANES
-    hops = partner_order(chips)[::-1]
-    for o in hops:
-        target = lax.rem(chip + o, chips)
-        grouped, rest = partial(target)
-        line = jnp.sum(rest * ones, 0, keepdims=True)
-        high = line.astype(jnp.bfloat16).astype(jnp.float32)
-        row = lax.broadcasted_iota(jnp.int32, (TAPS, LANES), 0)
-        lines = jnp.where(row == 0, high, jnp.where(row == 1, line - high, 0.0))
-        pieces = [grouped[:, at * LANES : (at + 1) * LANES] for at in range(blocks)]
-        sums_out[target] = jnp.concatenate(pieces + [lines], 0).astype(jnp.bfloat16)
-        sum_copy(chip, target).start()
-    grouped, rest = partial(chip)
-    fill_ramps(ramps, dms, first_bin, 12, SHARED // CHUNK)
-    for o in hops:
-        source = lax.rem(chip + o, chips)
-        sum_copy(source, source).wait_recv()
-        came = sums_in[source].astype(jnp.float32)
-        size = 2 * bins
-        pieces = [came[at * size : (at + 1) * size] for at in range(blocks)]
-        grouped += jnp.concatenate(pieces, 1)
-        line = came[blocks * size : blocks * size + 1] + came[blocks * size + 1 : blocks * size + 2]
-        rest += jnp.sum(line * ones, 1, keepdims=True)
-    real, imag = grouped[:bins], grouped[bins:]
-    upper = jnp.concatenate([real, -imag], 1)
-    lower = jnp.concatenate([imag, real], 1)
+        grouped, rest = group_units(spectra, matches, some)
+        for at in range(chips):
+            up, low = slice(at * size, (at + 1) * size), slice(some + at * size, some + (at + 1) * size)
+            own_sums = jnp.concatenate([grouped[up], grouped[low]], 0)
+            own_rest = jnp.concatenate([rest[up], rest[low]], 0)
+            kept_sums[part, at] = own_sums
+            kept_rest[part, at] = jnp.broadcast_to(own_rest, (2 * size, LANES))
+            line = jnp.sum(own_rest * ones, 0, keepdims=True)
+            high = line.astype(jnp.bfloat16).astype(jnp.float32)
+            row = lax.broadcasted_iota(jnp.int32, (TAPS, LANES), 0)
+            lines = jnp.where(row == 0, high, jnp.where(row == 1, line - high, 0.0))
+            pieces = [own_sums[:, lane * LANES : (lane + 1) * LANES] for lane in range(blocks)]
+            sums_out[part, at] = jnp.concatenate(pieces + [lines], 0).astype(jnp.bfloat16)
+        for o in hops:
+            sum_copy(part, chip, lax.rem(chip + o, chips)).start()
+    fill_ramps(ramps, dms, first_bin, 10, SHARED // CHUNK)
     rows = []
-    for at in range(bins):
-        left = jnp.concatenate([upper[at : at + 1], lower[at : at + 1]], 0)
-        total = jnp.dot(
-            left.astype(jnp.bfloat16), ramps[at], preferred_element_type=jnp.float32
-        )
-        re = total[0:1] + rest[at : at + 1]
-        im = total[1:2] + rest[bins + at : bins + at + 1]
-        rows.append((re * re + im * im) * (1.0 / CHANNELS))
+    for part in range(parts):
+        grouped, rest = kept_sums[part, chip], kept_rest[part, chip][:, 0:1]
+        for o in hops:
+            source = lax.rem(chip + o, chips)
+            sum_copy(part, source, source).wait_recv()
+            came = sums_in[part, source].astype(jnp.float32)
+            tall = 2 * size
+            pieces = [came[at * tall : (at + 1) * tall] for at in range(blocks)]
+            grouped += jnp.concatenate(pieces, 1)
+            line = came[blocks * tall : blocks * tall + 1]
+            line += came[blocks * tall + 1 : blocks * tall + 2]
+            rest += jnp.sum(line * ones, 1, keepdims=True)
+        real, imag = grouped[:size], grouped[size:]
+        upper = jnp.concatenate([real, -imag], 1)
+        lower = jnp.concatenate([imag, real], 1)
+        for at in range(size):
+            left = jnp.concatenate([upper[at : at + 1], lower[at : at + 1]], 0)
+            total = jnp.dot(
+                left.astype(jnp.bfloat16), ramps[part * size + at],
+                preferred_element_type=jnp.float32,
+            )
+            re = total[0:1] + rest[at : at + 1]
+            im = total[1:2] + rest[size + at : size + at + 1]
+            rows.append((re * re + im * im) * (1.0 / CHANNELS))
     turned = jnp.concatenate(rows, 0).T
     for target in range(members):
         power_out[target] = turned[target * kept : (target + 1) * kept]
@@ -460,11 +477,12 @@
     for o in order:
         target = lax.rem(me + o, members)
         power_copy(target, target).wait_send()
-    for slab in range(slabs):
-        pair_copy(slab).wait_send()
-    for o in hops:
-        target = lax.rem(chip + o, chips)
-        sum_copy(target, target).wait_send()
+    for part in range(parts):
+        for slab in range(slabs):
+            pair_copy(slab, part).wait_send()
+        for o in hops:
+            target = lax.rem(chip + o, chips)
+            sum_copy(part, target, target).wait_send()
 
     @pl.when(seg > 0)
     def _():
@@ -481,7 +499,9 @@
     own_len, width = raw_samples.shape
     bins, kept, wide = BINS // members, DMS // members, min(SLAB, width)
     slabs, rows = width // wide, KEPT + TAPS
-    swap = 2 * bins * (SHARED // LANES) + TAPS
+    parts = 2 if bins % (2 * TAPS) == 0 else 1
+    size = bins // parts
+    swap = 2 * size * (SHARED // LANES) + TAPS
     chips = members // 2
     time, channel, shrink, grow, tap, twiddle = tables(chips)
     units = channel_units.reshape(CHANNELS // LANES, LANES)
@@ -507,17 +527,20 @@
             pltpu.VMEM((2 * BINS, width), jnp.float32),
             pltpu.VMEM((2 * BINS, width), jnp.float32),
             pltpu.VMEM((2 * BINS, wide), jnp.float32),
-            pltpu.VMEM((slabs, 2, chips, bins, wide), jnp.bfloat16),
-            pltpu.VMEM((2, slabs, 2, chips, bins, wide), jnp.bfloat16),
+            pltpu.VMEM((slabs, parts, 2, chips, size, wide), jnp.bfloat16),
+            pltpu.VMEM((2, slabs, parts, 2, chips, size, wide), jnp.bfloat16),
             pltpu.VMEM((bins, 2 * SHARED, DMS), jnp.bfloat16),
             pltpu.VMEM((RADIX, INNER, SHARED), jnp.bfloat16),
-            pltpu.VMEM((RADIX * bins, 2 * INNER), jnp.float32),
-            pltpu.VMEM((chips, swap, LANES), jnp.bfloat16),
-            pltpu.VMEM((chips, swap, LANES), jnp.bfloat16),
+            pltpu.VMEM((RADIX * chips * size, 2 * INNER), jnp.float32),
+            pltpu.VMEM((parts, chips, 2 * size, SHARED), jnp.float32),
+            pltpu.VMEM((parts, chips, 2 * size, LANES), jnp.float32),
+            pltpu.VMEM((parts, chips, swap, LANES), jnp.bfloat16),
+            pltpu.VMEM((parts, chips, swap, LANES), jnp.bfloat16),
             pltpu.VMEM((members, kept, bins), jnp.float32),
             pltpu.VMEM((members, kept, bins), jnp.float32),
-            dma((7,)), dma((1 + slabs,)), dma((1 + slabs,)), dma((slabs,)), dma((slabs,)),
-            dma((chips,)), dma((chips,)), dma((members,)), dma((members,)),
+            dma((7,)), dma((1 + slabs,)), dma((1 + slabs,)),
+            dma((slabs, parts)), dma((slabs, parts)), dma((parts, chips)), dma((parts, chips)),
+            dma((members,)), dma((members,)),
         ],
         compiler_params=pltpu.CompilerParams(
             vmem_limit_bytes=56 * 2**20, collective_id=0, has_side_effects=True

time: 32 us -> 31.5 us (0.984)
  Pallas kernels: 31.2 us -> 30.7 us
    pallas_call x1, Pallas kernels: 31.2 us -> 30.7 us  [body(): pl.pallas_call(functools.partial(kernel, members, lax.axis_size('tm')), o...]
where the time goes in v4:
time: 31.5 us; the launch traced here: 31.3 us
  Pallas kernels  30.7 us (97%)
  local copies, waits for them, and re-layouts  0.62 us (2%)
    pallas_call x1, Pallas kernels, body(): pl.pallas_call(functools.partial(kernel, members, lax.axis_size('tm')), o...  30.7 us

profile of v4, /device:TPU:0, one launch (start us, length us, event | category | flops | bytes accessed | tf_op | source)
XLA Modules:
  0.0 31.3 jit_solution(12621204858592982737)
XLA Ops:
  0.0 30.7 %shard_map.100 = f32[32,256]{1,0:T(8,128)S(1)} custom-call(bf16[1536,512]{1,0:T(8,128)(2,1)} %raw.1, bf16[512,1536]{1,0:T(8,128)(2,1)} %constant.12.clone.time_hbm, bf16[512,512]{1,0:T(8,128)(2,1)} %constant.13.clone.channel_hbm, bf16[320,512]{1,0:T(8,128)(2,1)} %constant.14.clone.shrink_hbm, bf16[512,320]{1,0:T(8,128)(2,1)} %constant.15.clone.grow_hbm, ...), custom_call_target="tpu_custom_call" | custom-call | tf_op jit(solution)/shard_map/pallas_call | solution.py:511
  30.7 0.6 %copy.12 = f32[1,32,256]{2,1,0:T(8,128)} copy(f32[1,32,256]{2,1,0:T(8,128)S(1)} %bitcast.3) | data formatting | bytes 65536

commit v5 on v4

--- a/solution.py
+++ b/solution.py
@@ -22,6 +22,7 @@
 LANES = 128
 SLAB = 256
 KEPT = 160
+TILE = 8
 
 
 def band_basis():
@@ -72,8 +73,14 @@
     return parts
 
 
+def bin_order(chips):
+    groups = BINS // (2 * chips * TILE)
+    bins = np.arange(BINS).reshape(groups, chips, 2, TILE)
+    return bins.transpose(2, 1, 0, 3).reshape(-1)
+
+
 def tables(chips):
-    bins = np.arange(BINS)[:, None]
+    bins = bin_order(chips)[:, None]
     angle = 2 * np.pi * (bins * np.arange(DFT_LEN)[None, :] % DFT_LEN) / DFT_LEN
     time = np.concatenate([np.cos(angle), -np.sin(angle)], 0) / math.sqrt(DFT_LEN)
     basis = band_basis()
@@ -112,32 +119,41 @@
     return cosine, sine * x
 
 
+def phasor(phase):
+    quarter = phase >> 9
+    cosine, sine = unit_circle(phase & 511)
+    odd = (quarter & 1) == 1
+    swapped_cos = jnp.where(odd, -sine, cosine)
+    swapped_sin = jnp.where(odd, cosine, sine)
+    far = quarter >= 2
+    return jnp.where(far, -swapped_cos, swapped_cos), jnp.where(far, -swapped_sin, swapped_sin)
+
+
+def turn(real, imag, cosine, sine):
+    return real * cosine - imag * sine, imag * cosine + real * sine
+
+
 def fill_ramps(ramps, dms, first_bin, start, stop):
-    bins = ramps.shape[0]
+    groups = ramps.shape[0] // TILE
 
     @pl.loop(start, stop)
     def _(step):
         row = pl.multiple_of(step * CHUNK, CHUNK)
         units = lax.broadcasted_iota(jnp.int32, (CHUNK, DMS), 0) + (row + 1)
         delays = (units * dms[...]) >> 10
-        turn_cos, turn_sin = unit_circle(delays)
-        phase = (delays * first_bin) & (DFT_LEN - 1)
-        quarter = phase >> 9
-        cosine, sine = unit_circle(phase & 511)
-        odd = (quarter & 1) == 1
-        swapped_cos = jnp.where(odd, -sine, cosine)
-        swapped_sin = jnp.where(odd, cosine, sine)
-        far = quarter >= 2
-        cosine = jnp.where(far, -swapped_cos, swapped_cos)
-        sine = jnp.where(far, -swapped_sin, swapped_sin)
-        for at in range(bins):
-            ramps[at, pl.ds(row, CHUNK), :] = cosine.astype(jnp.bfloat16)
-            ramps[at, pl.ds(SHARED + row, CHUNK), :] = sine.astype(jnp.bfloat16)
-            if at + 1 < bins:
-                cosine, sine = (
-                    cosine * turn_cos - sine * turn_sin,
-                    sine * turn_cos + cosine * turn_sin,
-                )
+        step_cos, step_sin = unit_circle(delays)
+        group_cos, group_sin = phasor((delays * first_bin) & (DFT_LEN - 1))
+        if groups > 1:
+            jump_cos, jump_sin = phasor((delays * (BINS // groups)) & (DFT_LEN - 1))
+        for group in range(groups):
+            cosine, sine = group_cos, group_sin
+            for at in range(TILE):
+                ramps[group * TILE + at, pl.ds(row, CHUNK), :] = cosine.astype(jnp.bfloat16)
+                ramps[group * TILE + at, pl.ds(SHARED + row, CHUNK), :] = sine.astype(jnp.bfloat16)
+                if at + 1 < TILE:
+                    cosine, sine = turn(cosine, sine, step_cos, step_sin)
+            if group + 1 < groups:
+                group_cos, group_sin = turn(group_cos, group_sin, jump_cos, jump_sin)
 
 
 def dft(real, imag):
@@ -249,7 +265,7 @@
         pltpu.make_async_copy(channel_hbm, channel, local_sem.at[5]),
         pltpu.make_async_copy(twiddle_hbm.at[chip], twiddle, local_sem.at[6]),
     ]
-    for load in loads:
+    for load in loads[:2]:
         load.start()
 
     barrier = pltpu.get_barrier_semaphore()
@@ -272,8 +288,18 @@
             barrier, inc=1, device_id={"tm": seg + 1}, device_id_type=pl.DeviceIdType.MESH
         )
 
+    @pl.when(seg == 0)
+    def _():
+        for load in loads[2:]:
+            load.start()
+
     for load in loads[:2]:
         load.wait()
+
+    @pl.when(seg > 0)
+    def _():
+        for load in loads[2:]:
+            load.start()
 
     @pl.when(seg > 0)
     def _():
@@ -331,7 +357,7 @@
     spec[...] = jnp.dot(time[...], own[...], preferred_element_type=jnp.float32)
     loads[4].wait()
     fill_matches(matches, units)
-    first_bin = core * (BINS // 2) + chip * bins
+    first_bin = me * TILE
     fill_ramps(ramps, dms, first_bin, 0, 4)
 
     @pl.when(seg > 0)
@@ -416,7 +442,8 @@
         )
         grouped, rest = group_units(spectra, matches, some)
         for at in range(chips):
-            up, low = slice(at * size, (at + 1) * size), slice(some + at * size, some + (at + 1) * size)
+            up = slice(at * size, (at + 1) * size)
+            low = slice(some + at * size, some + (at + 1) * size)
             own_sums = jnp.concatenate([grouped[up], grouped[low]], 0)
             own_rest = jnp.concatenate([rest[up], rest[low]], 0)
             kept_sums[part, at] = own_sums
@@ -455,9 +482,12 @@
             re = total[0:1] + rest[at : at + 1]
             im = total[1:2] + rest[size + at : size + at + 1]
             rows.append((re * re + im * im) * (1.0 / CHANNELS))
-    turned = jnp.concatenate(rows, 0).T
+    powers = jnp.concatenate(rows, 0)
+    groups = bins // TILE
     for target in range(members):
-        power_out[target] = turned[target * kept : (target + 1) * kept]
+        cols = slice(target * kept, (target + 1) * kept)
+        pieces = [powers[at * TILE : (at + 1) * TILE, cols] for at in range(groups)]
+        power_out[target] = jnp.concatenate(pieces, 1)
 
     def power_copy(slot, target):
         return pltpu.make_async_remote_copy(
@@ -469,14 +499,6 @@
     for o in order:
         power_copy(me, lax.rem(me + o, members)).start()
     power_in[me] = power_out[me]
-    for o in order:
-        target = lax.rem(me + o, members)
-        power_copy(target, target).wait_recv()
-    sources = [2 * at + half for half in range(2) for at in range(chips)]
-    out[...] = jnp.concatenate([power_in[source] for source in sources], 1)
-    for o in order:
-        target = lax.rem(me + o, members)
-        power_copy(target, target).wait_send()
     for part in range(parts):
         for slab in range(slabs):
             pair_copy(slab, part).wait_send()
@@ -492,6 +514,15 @@
     @pl.when(seg < segments - 1)
     def _():
         forward_copy().wait_send()
+    for o in order:
+        target = lax.rem(me + o, members)
+        power_copy(target, target).wait_send()
+    for o in order:
+        target = lax.rem(me + o, members)
+        power_copy(target, target).wait_recv()
+    turned = jnp.concatenate([power_in[source] for source in range(members)], 0).T
+    pieces = [turned[at * kept : (at + 1) * kept] for at in range(groups)]
+    out[...] = jnp.concatenate(pieces, 1)
 
 
 def body(raw_samples, filter_taps, dm_trials, channel_units):
@@ -536,8 +567,8 @@
             pltpu.VMEM((parts, chips, 2 * size, LANES), jnp.float32),
             pltpu.VMEM((parts, chips, swap, LANES), jnp.bfloat16),
             pltpu.VMEM((parts, chips, swap, LANES), jnp.bfloat16),
-            pltpu.VMEM((members, kept, bins), jnp.float32),
-            pltpu.VMEM((members, kept, bins), jnp.float32),
+            pltpu.VMEM((members, TILE, bins // TILE * kept), jnp.float32),
+            pltpu.VMEM((members, TILE, bins // TILE * kept), jnp.float32),
             dma((7,)), dma((1 + slabs,)), dma((1 + slabs,)),
             dma((slabs, parts)), dma((slabs, parts)), dma((parts, chips)), dma((parts, chips)),
             dma((members,)), dma((members,)),

time: 31.5 us -> 29.8 us (0.946)
  Pallas kernels: 30.7 us -> 28.9 us
    pallas_call x1, Pallas kernels: 30.7 us -> 28.9 us  [body(): pl.pallas_call(functools.partial(kernel, members, lax.axis_size('tm')), o...]
where the time goes in v5:
time: 29.8 us; the launch traced here: 29.6 us
  Pallas kernels  28.9 us (97%)
  local copies, waits for them, and re-layouts  0.62 us (2%)
    pallas_call x1, Pallas kernels, body(): pl.pallas_call(functools.partial(kernel, members, lax.axis_size('tm')), o...  28.9 us
    unnamed x1, local copies, waits for them, and re-layouts  0.62 us

profile of v5, /device:TPU:0, one launch (start us, length us, event | category | flops | bytes accessed | tf_op | source)
XLA Modules:
  0.0 29.6 jit_solution(13804557351821397219)
XLA Ops:
  0.0 28.9 %shard_map.100 = f32[32,256]{1,0:T(8,128)S(1)} custom-call(bf16[1536,512]{1,0:T(8,128)(2,1)} %raw.1, bf16[512,1536]{1,0:T(8,128)(2,1)} %constant.12.clone.time_hbm, bf16[512,512]{1,0:T(8,128)(2,1)} %constant.13.clone.channel_hbm, bf16[320,512]{1,0:T(8,128)(2,1)} %constant.14.clone.shrink_hbm, bf16[512,320]{1,0:T(8,128)(2,1)} %constant.15.clone.grow_hbm, ...), custom_call_target="tpu_custom_call" | custom-call | tf_op jit(solution)/shard_map/pallas_call | solution.py:542
  28.9 0.6 %copy.12 = f32[1,32,256]{2,1,0:T(8,128)} copy(f32[1,32,256]{2,1,0:T(8,128)S(1)} %bitcast.3) | data formatting | bytes 65536

commit v6 on v5

--- a/solution.py
+++ b/solution.py
@@ -205,8 +205,10 @@
             k2 = r + stride * at
             c, s = twiddle[0, k2 : k2 + 1, :], twiddle[1, k2 : k2 + 1, :]
             rows = slice(k2 * bins, k2 * bins + bins)
-            first[rows, 0:INNER] = outs_real[at] * c - outs_imag[at] * s
-            first[rows, INNER:] = outs_real[at] * s + outs_imag[at] * c
+            value = outs_real[at] * c - outs_imag[at] * s
+            first[rows, 0:INNER] = value.astype(jnp.bfloat16)
+            value = outs_real[at] * s + outs_imag[at] * c
+            first[rows, INNER:] = value.astype(jnp.bfloat16)
 
 
 def fill_matches(matches, units):
@@ -220,14 +222,18 @@
 
 
 def group_units(spectra, matches, bins):
-    grouped = jnp.zeros((2 * bins, SHARED), jnp.float32)
     whole = jnp.zeros((2 * bins, INNER), jnp.float32)
+    pieces = []
     for k2 in range(RADIX):
         part = spectra[k2 * bins : (k2 + 1) * bins]
         part = jnp.concatenate([part[:, :INNER], part[:, INNER:]], 0)
         part = part.astype(jnp.bfloat16)
         whole += part.astype(jnp.float32)
-        grouped += jnp.dot(part, matches[k2], preferred_element_type=jnp.float32)
+        pieces.append(part)
+    grouped = jnp.dot(
+        jnp.concatenate(pieces, 1), matches[...].reshape(CHANNELS, SHARED),
+        preferred_element_type=jnp.float32,
+    )
     rest = jnp.sum(whole, 1, keepdims=True) - jnp.sum(grouped, 1, keepdims=True)
     return grouped, rest
 
@@ -270,10 +276,10 @@
 
     barrier = pltpu.get_barrier_semaphore()
     order = partner_order(members)
-    for o in order:
+    near = [lax.rem(me + 2 * o, members) for o in range(1, chips)] + [me + 1 - 2 * core]
+    for peer in near:
         pl.semaphore_signal(
-            barrier, inc=1, device_id={"freq": lax.rem(me + o, members)},
-            device_id_type=pl.DeviceIdType.MESH,
+            barrier, inc=1, device_id={"freq": peer}, device_id_type=pl.DeviceIdType.MESH
         )
 
     @pl.when(seg > 0)
@@ -311,7 +317,7 @@
             edges[slab, KEPT:, :] = own[SHARED - TAPS : SHARED, cols]
 
     pl.semaphore_wait(
-        barrier, members - 1 + jnp.minimum(seg, 1) + jnp.minimum(segments - 1 - seg, 1)
+        barrier, len(near) + jnp.minimum(seg, 1) + jnp.minimum(segments - 1 - seg, 1)
     )
 
     def back_copy(slab):
@@ -422,8 +428,9 @@
         load.wait()
 
     def sum_copy(part, slot, target):
+        sent = pl.ds(0, sums_in.shape[2] - (TAPS if part + 1 < parts else 0))
         return pltpu.make_async_remote_copy(
-            src_ref=sums_out.at[part, target], dst_ref=sums_in.at[part, slot],
+            src_ref=sums_out.at[part, target, sent], dst_ref=sums_in.at[part, slot, sent],
             send_sem=sum_send.at[part, target], recv_sem=sum_recv.at[part, slot],
             device_id={"freq": 2 * target + core}, device_id_type=pl.DeviceIdType.MESH,
         )
@@ -433,12 +440,15 @@
     blocks = SHARED // LANES
     hops = partner_order(chips)[::-1]
     some = chips * size
+    tall = 2 * size
+    line_row = lax.broadcasted_iota(jnp.int32, (TAPS, LANES), 0)
+    lines = [jnp.zeros((TAPS, LANES), jnp.float32)] * chips
     for part in range(parts):
         for slab in range(slabs):
             pair_copy(slab, part).wait_recv()
         channelize(pair, twiddle, first, part)
         spectra = jnp.dot(
-            first[...].astype(jnp.bfloat16), channel[...], preferred_element_type=jnp.float32
+            first[...], channel[...], preferred_element_type=jnp.float32
         )
         grouped, rest = group_units(spectra, matches, some)
         for at in range(chips):
@@ -450,44 +460,58 @@
             kept_rest[part, at] = jnp.broadcast_to(own_rest, (2 * size, LANES))
             line = jnp.sum(own_rest * ones, 0, keepdims=True)
             high = line.astype(jnp.bfloat16).astype(jnp.float32)
-            row = lax.broadcasted_iota(jnp.int32, (TAPS, LANES), 0)
-            lines = jnp.where(row == 0, high, jnp.where(row == 1, line - high, 0.0))
+            lines[at] = jnp.where(line_row == 2 * part, high, lines[at])
+            lines[at] = jnp.where(line_row == 2 * part + 1, line - high, lines[at])
             pieces = [own_sums[:, lane * LANES : (lane + 1) * LANES] for lane in range(blocks)]
-            sums_out[part, at] = jnp.concatenate(pieces + [lines], 0).astype(jnp.bfloat16)
+            pieces = jnp.concatenate(pieces, 0).astype(jnp.bfloat16)
+            sums_out[part, at, 0 : blocks * tall, :] = pieces
+            if part + 1 == parts:
+                sums_out[part, at, blocks * tall :, :] = lines[at].astype(jnp.bfloat16)
         for o in hops:
             sum_copy(part, chip, lax.rem(chip + o, chips)).start()
     fill_ramps(ramps, dms, first_bin, 10, SHARED // CHUNK)
-    rows = []
+    totals = []
+    tile_row = lax.broadcasted_iota(jnp.int32, (TILE, DMS), 0)
     for part in range(parts):
-        grouped, rest = kept_sums[part, chip], kept_rest[part, chip][:, 0:1]
+        grouped = kept_sums[part, chip]
         for o in hops:
             source = lax.rem(chip + o, chips)
             sum_copy(part, source, source).wait_recv()
-            came = sums_in[part, source].astype(jnp.float32)
-            tall = 2 * size
+            came = sums_in[part, source, 0 : blocks * tall, :].astype(jnp.float32)
             pieces = [came[at * tall : (at + 1) * tall] for at in range(blocks)]
             grouped += jnp.concatenate(pieces, 1)
-            line = came[blocks * tall : blocks * tall + 1]
-            line += came[blocks * tall + 1 : blocks * tall + 2]
-            rest += jnp.sum(line * ones, 1, keepdims=True)
         real, imag = grouped[:size], grouped[size:]
         upper = jnp.concatenate([real, -imag], 1)
         lower = jnp.concatenate([imag, real], 1)
-        for at in range(size):
-            left = jnp.concatenate([upper[at : at + 1], lower[at : at + 1]], 0)
-            total = jnp.dot(
-                left.astype(jnp.bfloat16), ramps[part * size + at],
-                preferred_element_type=jnp.float32,
-            )
-            re = total[0:1] + rest[at : at + 1]
-            im = total[1:2] + rest[size + at : size + at + 1]
-            rows.append((re * re + im * im) * (1.0 / CHANNELS))
-    powers = jnp.concatenate(rows, 0)
-    groups = bins // TILE
+        for group in range(size // TILE):
+            tile = slice(group * TILE, (group + 1) * TILE)
+            left = jnp.concatenate([upper[tile], lower[tile]], 0).astype(jnp.bfloat16)
+            re = jnp.zeros((TILE, DMS), jnp.float32)
+            im = jnp.zeros((TILE, DMS), jnp.float32)
+            for at in range(TILE):
+                total = jnp.dot(
+                    left, ramps[part * size + group * TILE + at],
+                    preferred_element_type=jnp.float32,
+                )
+                re = jnp.where(tile_row == at, total[:TILE], re)
+                im = jnp.where(tile_row == at, total[TILE:], im)
+            totals.append((re, im))
+    powers = []
+    for part in range(parts):
+        rest = kept_rest[part, chip][:, 0:1]
+        for o in hops:
+            source = lax.rem(chip + o, chips)
+            line = sums_in[parts - 1, source, blocks * tall :, :].astype(jnp.float32)
+            line = line[2 * part : 2 * part + 1] + line[2 * part + 1 : 2 * part + 2]
+            rest += jnp.sum(line * ones, 1, keepdims=True)
+        for group in range(size // TILE):
+            re, im = totals[part * (size // TILE) + group]
+            re += rest[group * TILE : (group + 1) * TILE]
+            im += rest[size + group * TILE : size + (group + 1) * TILE]
+            powers.append((re * re + im * im) * (1.0 / CHANNELS))
     for target in range(members):
         cols = slice(target * kept, (target + 1) * kept)
-        pieces = [powers[at * TILE : (at + 1) * TILE, cols] for at in range(groups)]
-        power_out[target] = jnp.concatenate(pieces, 1)
+        power_out[target] = jnp.concatenate([power[:, cols] for power in powers], 1)
 
     def power_copy(slot, target):
         return pltpu.make_async_remote_copy(
@@ -521,7 +545,7 @@
         target = lax.rem(me + o, members)
         power_copy(target, target).wait_recv()
     turned = jnp.concatenate([power_in[source] for source in range(members)], 0).T
-    pieces = [turned[at * kept : (at + 1) * kept] for at in range(groups)]
+    pieces = [turned[at * kept : (at + 1) * kept] for at in range(bins // TILE)]
     out[...] = jnp.concatenate(pieces, 1)
 
 
@@ -562,7 +586,7 @@
             pltpu.VMEM((2, slabs, parts, 2, chips, size, wide), jnp.bfloat16),
             pltpu.VMEM((bins, 2 * SHARED, DMS), jnp.bfloat16),
             pltpu.VMEM((RADIX, INNER, SHARED), jnp.bfloat16),
-            pltpu.VMEM((RADIX * chips * size, 2 * INNER), jnp.float32),
+            pltpu.VMEM((RADIX * chips * size, 2 * INNER), jnp.bfloat16),
             pltpu.VMEM((parts, chips, 2 * size, SHARED), jnp.float32),
             pltpu.VMEM((parts, chips, 2 * size, LANES), jnp.float32),
             pltpu.VMEM((parts, chips, swap, LANES), jnp.bfloat16),

time: 29.8 us -> 29.1 us (0.977)
  Pallas kernels: 28.9 us -> 28.3 us
    pallas_call x1, Pallas kernels: 28.9 us -> 28.3 us  [body(): pl.pallas_call(functools.partial(kernel, members, lax.axis_size('tm')), o...]
where the time goes in v6:
time: 29.1 us; the launch traced here: 28.9 us
  Pallas kernels  28.3 us (97%)
  local copies, waits for them, and re-layouts  0.62 us (2%)
    pallas_call x1, Pallas kernels, body(): pl.pallas_call(functools.partial(kernel, members, lax.axis_size('tm')), o...  28.3 us
    unnamed x1, local copies, waits for them, and re-layouts  0.62 us

profile of v6, /device:TPU:0, one launch (start us, length us, event | category | flops | bytes accessed | tf_op | source)
XLA Modules:
  0.0 28.9 jit_solution(18235034161889161729)
XLA Ops:
  0.0 28.3 %shard_map.100 = f32[32,256]{1,0:T(8,128)S(1)} custom-call(bf16[1536,512]{1,0:T(8,128)(2,1)} %raw.1, bf16[512,1536]{1,0:T(8,128)(2,1)} %constant.12.clone.time_hbm, bf16[512,512]{1,0:T(8,128)(2,1)} %constant.13.clone.channel_hbm, bf16[320,512]{1,0:T(8,128)(2,1)} %constant.14.clone.shrink_hbm, bf16[512,320]{1,0:T(8,128)(2,1)} %constant.15.clone.grow_hbm, ...), custom_call_target="tpu_custom_call" | custom-call | tf_op jit(solution)/shard_map/pallas_call | solution.py:566
  28.3 0.6 %copy.12 = f32[1,32,256]{2,1,0:T(8,128)} copy(f32[1,32,256]{2,1,0:T(8,128)S(1)} %bitcast.3) | data formatting | bytes 65536

commit v7 on v6

--- a/solution.py
+++ b/solution.py
@@ -120,12 +120,19 @@
 
 
 def phasor(phase):
-    quarter = phase >> 9
-    cosine, sine = unit_circle(phase & 511)
+    quarter = (phase + 256) >> 9
+    x = (phase - (quarter << 9)).astype(jnp.float32) * (2.0 * math.pi / DFT_LEN)
+    y = x * x
+    sine, cosine = jnp.full_like(y, 1 / 362880), jnp.full_like(y, 1 / 40320)
+    for value in (-1 / 5040, 1 / 120, -1 / 6, 1.0):
+        sine = sine * y + value
+    for value in (-1 / 720, 1 / 24, -0.5, 1.0):
+        cosine = cosine * y + value
+    sine = sine * x
     odd = (quarter & 1) == 1
     swapped_cos = jnp.where(odd, -sine, cosine)
     swapped_sin = jnp.where(odd, cosine, sine)
-    far = quarter >= 2
+    far = (quarter & 2) == 2
     return jnp.where(far, -swapped_cos, swapped_cos), jnp.where(far, -swapped_sin, swapped_sin)
 
 
@@ -142,16 +149,22 @@
         units = lax.broadcasted_iota(jnp.int32, (CHUNK, DMS), 0) + (row + 1)
         delays = (units * dms[...]) >> 10
         step_cos, step_sin = unit_circle(delays)
+        double = step_cos + step_cos
         group_cos, group_sin = phasor((delays * first_bin) & (DFT_LEN - 1))
         if groups > 1:
             jump_cos, jump_sin = phasor((delays * (BINS // groups)) & (DFT_LEN - 1))
         for group in range(groups):
             cosine, sine = group_cos, group_sin
+            next_cos, next_sin = turn(cosine, sine, step_cos, step_sin)
             for at in range(TILE):
                 ramps[group * TILE + at, pl.ds(row, CHUNK), :] = cosine.astype(jnp.bfloat16)
                 ramps[group * TILE + at, pl.ds(SHARED + row, CHUNK), :] = sine.astype(jnp.bfloat16)
-                if at + 1 < TILE:
-                    cosine, sine = turn(cosine, sine, step_cos, step_sin)
+                if at + 2 < TILE:
+                    last_cos, last_sin = cosine, sine
+                    cosine, sine = next_cos, next_sin
+                    next_cos, next_sin = double * cosine - last_cos, double * sine - last_sin
+                else:
+                    cosine, sine = next_cos, next_sin
             if group + 1 < groups:
                 group_cos, group_sin = turn(group_cos, group_sin, jump_cos, jump_sin)
 

time: 29.1 us -> 28.8 us (0.990)
  Pallas kernels: 28.3 us -> 28 us
    pallas_call x1, Pallas kernels: 28.3 us -> 28 us  [body(): pl.pallas_call(functools.partial(kernel, members, lax.axis_size('tm')), o...]
where the time goes in v7:
time: 28.8 us; the launch traced here: 28.6 us
  Pallas kernels  28 us (97%)
  local copies, waits for them, and re-layouts  0.62 us (2%)
    pallas_call x1, Pallas kernels, body(): pl.pallas_call(functools.partial(kernel, members, lax.axis_size('tm')), o...  28 us
    unnamed x1, local copies, waits for them, and re-layouts  0.62 us

profile of v7, /device:TPU:0, one launch (start us, length us, event | category | flops | bytes accessed | tf_op | source)
XLA Modules:
  0.0 28.6 jit_solution(8124601807216479808)
XLA Ops:
  0.0 28.0 %shard_map.100 = f32[32,256]{1,0:T(8,128)S(1)} custom-call(bf16[1536,512]{1,0:T(8,128)(2,1)} %raw.1, bf16[512,1536]{1,0:T(8,128)(2,1)} %constant.12.clone.time_hbm, bf16[512,512]{1,0:T(8,128)(2,1)} %constant.13.clone.channel_hbm, bf16[320,512]{1,0:T(8,128)(2,1)} %constant.14.clone.shrink_hbm, bf16[512,320]{1,0:T(8,128)(2,1)} %constant.15.clone.grow_hbm, ...), custom_call_target="tpu_custom_call" | custom-call | tf_op jit(solution)/shard_map/pallas_call | solution.py:579
  28.0 0.6 %copy.12 = f32[1,32,256]{2,1,0:T(8,128)} copy(f32[1,32,256]{2,1,0:T(8,128)S(1)} %bitcast.3) | data formatting | bytes 65536
